TPU v7x, 32 devices: a whole 2x2x4 slice. The times are simulated.
32 devices in a mesh: fsdp: 8 (over y, x, core), rep: 4 (over z).
Axes of the slice: x: 2, y: 2, z: 4, core: 2. Of those that a mesh axis runs over, the one named last changes fastest.
Arguments:
- grads: bfloat16 [8, 1024, 1024], P('rep', 'fsdp'), may hold values from -6 to 6
- second_moment: bfloat16 [8, 1024, 1024], P('rep', 'fsdp'), may hold values from 0.0099487305 to 1
- root_factors: bfloat16 [4, 8, 1024, 1024], P('rep', 'fsdp')
- block_shape: int32 [8, 2], replicated, may hold values from 128 to 1024, as said below
- block_owner: int32 [8], replicated, may hold values from 0 to 7, as said below
Outputs:
- direction: bfloat16 [8, 1024, 1024], P('rep', 'fsdp')
Inputs may be any that keep to these rules, and one draw needn't show every extreme that they name: `block_owner`: the 4 blocks of rep indices 2k and 2k+1 have distinct owners. `block_shape`: each entry is 1024 or a tail of at least 128.
All inputs are finite; a program needn't handle non-finite values.
Results may differ from a plain program's by a relative error of at most 0.0057.
Values may be sent and summed in bfloat16 or wider, within the bound.
A program may use at most 64 MiB of HBM per device.

v0:
```python
import jax
import jax.numpy as jnp
from jax import lax
from jax.sharding import PartitionSpec as P

ADAM_EPS = 1e-08
NORM_EPS = 1e-06


def shifted(block, axis, distance):
    devices = range(lax.axis_size(axis))
    route = [(i - distance, i) for i in devices if i - distance in devices]
    return lax.ppermute(block, axis, route)


def on_device(grads, second_moment, root_factors, block_shape, block_owner):
    count = grads.shape[0]
    band = grads.shape[1]
    width = grads.shape[2]
    total_ids = block_shape.shape[0]
    owners = lax.axis_size("fsdp")
    fsdp_at = lax.axis_index("fsdp")
    rep_at = lax.axis_index("rep")
    parity = rep_at % 2
    first_id = rep_at * count
    local_ids = first_id + jnp.arange(count, dtype=jnp.int32)
    local_shape = lax.dynamic_slice_in_dim(block_shape, first_id, count, 0)
    row_index = fsdp_at * band + jnp.arange(band, dtype=jnp.int32)
    col_index = jnp.arange(width, dtype=jnp.int32)
    inside = (row_index[None, :, None] < local_shape[:, 0][:, None, None]) & (
        col_index[None, None, :] < local_shape[:, 1][:, None, None]
    )
    masked = jnp.where(inside, grads, jnp.zeros_like(grads))
    adam = masked.astype(jnp.float32) / (jnp.sqrt(second_moment.astype(jnp.float32)) + ADAM_EPS)
    adam_part = jnp.sum(adam * adam, axis=(1, 2))
    spread = lax.dynamic_update_slice_in_dim(
        jnp.zeros((total_ids,), jnp.float32), adam_part, first_id, 0
    )
    adam_all = lax.psum(spread, ("fsdp", "rep"))
    factor = root_factors[0, 0]
    partner = shifted(masked, "rep", -1)
    pair_start = rep_at // 2 * (2 * count)
    pair_owner = lax.dynamic_slice_in_dim(block_owner, pair_start, 2 * count, 0)
    pair_shape = lax.dynamic_slice_in_dim(block_shape, pair_start, 2 * count, 0)
    pair_grads = jnp.concatenate([masked, partner], axis=0)
    slot_hit = jnp.arange(owners, dtype=jnp.int32)[:, None] == pair_owner[None, :]
    placing = jnp.where(parity == 0, slot_hit, False).astype(jnp.bfloat16)
    outbound = jnp.einsum(
        "ob,brc->orc", placing, pair_grads, preferred_element_type=jnp.float32
    ).astype(jnp.bfloat16)
    inbound = lax.all_to_all(outbound, "fsdp", split_axis=0, concat_axis=1, tiled=True)
    gathered = inbound.reshape(width, width)

    def nothing():
        return jnp.zeros((width, width), jnp.bfloat16)

    def right_product():
        return jnp.dot(gathered, factor, preferred_element_type=jnp.float32).astype(jnp.bfloat16)

    halfway = lax.cond(parity == 0, right_product, nothing)
    arrived = shifted(halfway, "rep", 1)
    team_hit = pair_owner == fsdp_at
    team_shape = jnp.sum(jnp.where(team_hit[:, None], pair_shape, 0), axis=0)
    square = (col_index[:, None] < team_shape[0]) & (col_index[None, :] < team_shape[1])

    def left_product():
        full = jnp.dot(factor, arrived, preferred_element_type=jnp.float32)
        return jnp.where(square, full, jnp.zeros_like(full)).astype(jnp.bfloat16)

    product = lax.cond(parity == 1, left_product, nothing)
    product_wide = product.astype(jnp.float32)
    product_sq = jnp.sum(product_wide * product_wide)
    returned = lax.all_to_all(
        product.reshape(owners, band, width), "fsdp", split_axis=0, concat_axis=0, tiled=True
    )
    picking = slot_hit.T.astype(jnp.bfloat16)
    picked = jnp.einsum(
        "bo,orc->brc", picking, returned, preferred_element_type=jnp.float32
    ).astype(jnp.bfloat16)
    moved = shifted(picked[:count], "rep", -1)
    result = jnp.where(parity == 1, picked[count:], moved)
    own_square = jnp.where(team_hit & (parity == 1), product_sq, 0.0)
    spread_sq = lax.dynamic_update_slice_in_dim(
        jnp.zeros((total_ids,), jnp.float32), own_square, pair_start, 0
    )
    shampoo_all = lax.psum(spread_sq, ("fsdp", "rep"))
    local_adam = jnp.take(adam_all, local_ids)
    local_shampoo = jnp.take(shampoo_all, local_ids)
    scaling_local = jnp.sqrt(local_adam) / jnp.sqrt(local_shampoo + NORM_EPS)
    direction = (result.astype(jnp.float32) * scaling_local[:, None, None]).astype(jnp.bfloat16)
    return direction


def solution(mesh):
    placed = (
        P("rep", "fsdp", None),
        P("rep", "fsdp", None),
        P("rep", "fsdp", None, None),
        P(),
        P(),
    )
    return jax.shard_map(
        on_device, mesh=mesh, in_specs=placed, out_specs=P("rep", "fsdp", None), check_vma=False
    )
```

profile of v0, /device:TPU:0, one launch (start us, length us, event | category | flops | bytes accessed | tf_op | source)
XLA Modules:
  0.0 191.7 jit_solution(2981389652153336553)
XLA Ops:
  0.0 0.7 constant_dynamic-slice_fusion
  0.8 0.1 iota_compare_fusion
  0.8 0.1 broadcast_compare_fusion
  0.9 1.9 multiply_reduce_fusion.1
  2.8 1.3 collective-permute-start
  4.1 0.7 broadcast_compare_fusion.1
  4.9 14.8 %collective-permute-done = bf16[2,128,1024]{2,1,0:T(8,128)(2,1)S(1)} collective-permute-done((bf16[2,128,1024]{2,1,0:T(8,128)(2,1)S(1)}, bf16[2,128,1024]{2,1,0:T(8,128)(2,1)S(1)}, u32[]{:S(2)}, u32[]{:S(2)}) %collective-permute-start) | collective-permute-done | bytes 524320 | tf_op jit(solution)/shard_map/ppermute | solution.py:13
  19.7 0.1 pad_maximum_fusion
  19.8 1.3 convolution_convert_fusion.1
  21.0 2.5 %copy.21 = bf16[8,128,1024]{2,1,0:T(8,128)(2,1)} copy(bf16[8,128,1024]{2,0,1:T(8,128)(2,1)S(1)} %convolution_convert_fusion.1) | data formatting | bytes 4194304 | tf_op jit(solution)/shard_map/convert_element_type | solution.py:50
  23.5 3.9 %all-to-all-start = ((bf16[8,128,1024]{2,1,0:T(8,128)(2,1)}), bf16[8,128,1024]{2,1,0:T(8,128)(2,1)S(1)}, u32[]{:S(2)}, u32[]{:S(2)}) async-start(bf16[8,128,1024]{2,1,0:T(8,128)(2,1)} %copy.21), calls=%async_computation | async-start | bytes 4194304 | tf_op jit(solution)/shard_map/all_to_all | solution.py:51
  27.4 26.6 %all-to-all-done = bf16[8,128,1024]{2,1,0:T(8,128)(2,1)S(1)} async-done(((bf16[8,128,1024]{2,1,0:T(8,128)(2,1)}), bf16[8,128,1024]{2,1,0:T(8,128)(2,1)S(1)}, u32[]{:S(2)}, u32[]{:S(2)}) %all-to-all-start) | async-done | bytes 2097184 | tf_op jit(solution)/shard_map/all_to_all | solution.py:51
  54.1 0.0 copy-start.1
  54.1 5.9 %conditional.2 = (bf16[1024,1024]{1,0:T(8,128)(2,1)S(1)}) conditional(s32[]{:T(128)} %convert_element_type.37, () %tuple.21, (bf16[8,128,1024]{2,1,0:T(8,128)(2,1)S(1)}, bf16[1024,1024]{1,0:T(8,128)(2,1)}) %tuple.35), branch_computations={%region_0.1_spmd, %region_1.2_spmd} | conditional | flops 2148532224 | bytes 14680100 | solution.py:60
  54.1 0.0 copy-start
  54.1 1.3 copy-done
  55.4 4.5 %convolution_convert_fusion = bf16[1024,1024]{1,0:T(8,128)(2,1)S(1)} fusion(bf16[1024,1024]{1,0:T(8,128)(2,1)} %bitcast.19, bf16[1024,1024]{1,0:T(8,128)(2,1)} %get-tuple-element.73), kind=kOutput, calls=%fused_computation.2 | convolution fusion | flops 2148532224 | bytes 6291456 | tf_op jit(solution)/shard_map/cond/branch_1_fun/dot_general | solution.py:58
  60.0 2.6 %collective-permute-start.1 = (bf16[1024,1024]{1,0:T(8,128)(2,1)S(1)}, bf16[1024,1024]{1,0:T(8,128)(2,1)}, u32[]{:S(2)}, u32[]{:S(2)}) collective-permute-start(bf16[1024,1024]{1,0:T(8,128)(2,1)S(1)} %get-tuple-element.95), channel_id=1, source_target_pairs={{0,1},{1,2},{2,3},{4,5},{5,6},{6,7},{8,9},{9,10},{10,11},{12,13},{... | collective-permute-start | bytes 6291464 | tf_op jit(solution)/shard_map/ppermute | solution.py:13
  62.6 41.0 %collective-permute-done.1 = bf16[1024,1024]{1,0:T(8,128)(2,1)} collective-permute-done((bf16[1024,1024]{1,0:T(8,128)(2,1)S(1)}, bf16[1024,1024]{1,0:T(8,128)(2,1)}, u32[]{:S(2)}, u32[]{:S(2)}) %collective-permute-start.1) | collective-permute-done | bytes 2097184 | tf_op jit(solution)/shard_map/ppermute | solution.py:13
  103.7 0.0 copy-done.1
  103.7 1.6 conditional.3
  103.7 1.6 broadcast.76
  105.2 4.8 %all-to-all-start.1 = ((bf16[8,128,1024]{2,1,0:T(8,128)(2,1)}), bf16[8,128,1024]{2,1,0:T(8,128)(2,1)S(1)}, u32[]{:S(2)}, u32[]{:S(2)}) async-start(bf16[8,128,1024]{2,1,0:T(8,128)(2,1)} %bitcast.8), calls=%async_computation.1 | async-start | bytes 4194304 | tf_op jit(solution)/shard_map/all_to_all | solution.py:73
  110.1 0.2 dynamic_update_slice.6
  110.3 3.3 %multiply_reduce_fusion = f32[]{:T(128)} fusion(bf16[1024,1024]{1,0:T(8,128)(2,1)} %get-tuple-element.96), kind=kLoop, calls=%fused_computation.7 | loop fusion | flops 3145727 | bytes 2097156 | tf_op jit(solution)/shard_map/reduce_sum | solution.py:72
  113.6 23.1 %all-to-all-done.1 = bf16[8,128,1024]{2,1,0:T(8,128)(2,1)S(1)} async-done(((bf16[8,128,1024]{2,1,0:T(8,128)(2,1)}), bf16[8,128,1024]{2,1,0:T(8,128)(2,1)S(1)}, u32[]{:S(2)}, u32[]{:S(2)}) %all-to-all-start.1) | async-done | bytes 2097184 | tf_op jit(solution)/shard_map/all_to_all | solution.py:73
  136.7 1.4 fusion
  138.2 0.3 copy.29
  138.5 1.3 collective-permute-start.2
  139.8 0.7 fusion.12
  140.6 48.8 %all-reduce = (f32[8]{0:T(128)S(1)}, f32[8]{0:T(128)S(1)}) all-reduce(f32[8]{0:T(128)S(1)} %fusion.12, f32[8]{0:T(128)S(1)} %dynamic_update_slice.6), channel_id=1, replica_groups=mesh['fsdp'=8,'rep'=4] {'fsdp','rep'}, use_global_device_ids=true, to_apply=%region_8.10 | all-reduce | flops 16 | bytes 128 | tf_op jit(solution)/shard_map/psum | solution.py:86
  189.4 0.6 gather_fusion
  190.1 0.6 gather_fusion.1
  190.7 0.0 collective-permute-done.2
  190.7 1.0 multiply_convert_fusion
  (10 shorter events, 0.1 us)
Async XLA Ops:
  2.8 16.8 %collective-permute-start = (bf16[2,128,1024]{2,1,0:T(8,128)(2,1)S(1)}, bf16[2,128,1024]{2,1,0:T(8,128)(2,1)S(1)}, u32[]{:S(2)}, u32[]{:S(2)}) collective-permute-start(bf16[2,128,1024]{2,1,0:T(8,128)(2,1)S(1)} %get-tuple-element.88), channel_id=1, source_target_pairs={{1,0},{2,1},{3,2},{5,4},{6,5},{7,6},{9,8},{10,9},{11,10},{13,12},{... | collective-permute-start | bytes 1572872 | tf_op jit(solution)/shard_map/ppermute | solution.py:13
  23.5 30.5 %all-to-all-start = ((bf16[8,128,1024]{2,1,0:T(8,128)(2,1)}), bf16[8,128,1024]{2,1,0:T(8,128)(2,1)S(1)}, u32[]{:S(2)}, u32[]{:S(2)}) async-start(bf16[8,128,1024]{2,1,0:T(8,128)(2,1)} %copy.21), calls=%async_computation | async-start | bytes 4194304 | tf_op jit(solution)/shard_map/all_to_all | solution.py:51
  54.1 49.6 %copy-start.1 = (s32[8,2]{0,1:T(2,128)S(1)}, s32[8,2]{0,1:T(2,128)}, u32[]{:S(2)}) copy-start(s32[8,2]{0,1:T(2,128)} %param.14) | copy-start | bytes 196
  54.1 1.3 copy-start
  60.0 43.7 %collective-permute-start.1 = (bf16[1024,1024]{1,0:T(8,128)(2,1)S(1)}, bf16[1024,1024]{1,0:T(8,128)(2,1)}, u32[]{:S(2)}, u32[]{:S(2)}) collective-permute-start(bf16[1024,1024]{1,0:T(8,128)(2,1)S(1)} %get-tuple-element.95), channel_id=1, source_target_pairs={{0,1},{1,2},{2,3},{4,5},{5,6},{6,7},{8,9},{9,10},{10,11},{12,13},{... | collective-permute-start | bytes 6291464 | tf_op jit(solution)/shard_map/ppermute | solution.py:13
  105.2 31.5 %all-to-all-start.1 = ((bf16[8,128,1024]{2,1,0:T(8,128)(2,1)}), bf16[8,128,1024]{2,1,0:T(8,128)(2,1)S(1)}, u32[]{:S(2)}, u32[]{:S(2)}) async-start(bf16[8,128,1024]{2,1,0:T(8,128)(2,1)} %bitcast.8), calls=%async_computation.1 | async-start | bytes 4194304 | tf_op jit(solution)/shard_map/all_to_all | solution.py:73
  138.5 52.2 %collective-permute-start.2 = (bf16[2,128,1024]{2,1,0:T(8,128)(2,1)S(1)}, bf16[2,128,1024]{2,1,0:T(8,128)(2,1)S(1)}, u32[]{:S(2)}, u32[]{:S(2)}) collective-permute-start(bf16[2,128,1024]{2,1,0:T(8,128)(2,1)S(1)} %slice.34), channel_id=1, source_target_pairs={{1,0},{2,1},{3,2},{5,4},{6,5},{7,6},{9,8},{10,9},{11,10},{13,12},{... | collective-permute-start | bytes 1572872 | tf_op jit(solution)/shard_map/ppermute | solution.py:13
where the time goes:
time: 192 us
  waiting for transfers between devices  106 us (55%)
  blocking collectives  48.8 us (25%)
  starting transfers between devices  13.9 us (7%)
  local copies, waits for them, and re-layouts  8.05 us (4%)
  other arithmetic  7.96 us (4%)
  matrix products  7.27 us (4%)
    ppermute x3, waiting for transfers between devices, shifted(): return lax.ppermute(block, axis, route)  55.8 us
    psum x1, blocking collectives, on_device(): shampoo_all = lax.psum(spread_sq, ('fsdp', 'rep'))  48.8 us
    all_to_all x1, waiting for transfers between devices, on_device(): lax.all_to_all(outbound, 'fsdp', split_axis=0, concat_axis=1, tiled=True)  26.6 us
    all_to_all x1, waiting for transfers between devices, on_device(): lax.all_to_all(product.reshape(owners, band, width), 'fsdp', split_axis=0...  23.1 us
    ppermute x3, starting transfers between devices, shifted(): return lax.ppermute(block, axis, route)  5.23 us
    all_to_all x1, starting transfers between devices, on_device(): lax.all_to_all(product.reshape(owners, band, width), 'fsdp', split_axis=0...  4.81 us
    dot_general x1, matrix products, right_product(): jnp.dot(gathered, factor, preferred_element_type=jnp.float32)  4.55 us
    all_to_all x1, starting transfers between devices, on_device(): lax.all_to_all(outbound, 'fsdp', split_axis=0, concat_axis=1, tiled=True)  3.88 us
  transfers between devices with their start and end apart: 5, of which 4 were waited for; matrix products, arithmetic and copies ran while one was open for 3% of the time, Pallas kernels for 0%

commit v1 on v0

v1 whole, which is shorter than its diff:
```python
import functools

import jax
import jax.numpy as jnp
from jax import lax
from jax.experimental import pallas as pl
from jax.experimental.pallas import tpu as pltpu
from jax.sharding import PartitionSpec as P

ADAM_EPS = 1e-08
NORM_EPS = 1e-06
MESH = pl.DeviceIdType.MESH


def flipped(index, mask, extent):
    out, bit = 0, 1
    while bit < extent:
        out = out + bit * (((index // bit) % 2 + (mask // bit) % 2) % 2)
        bit *= 2
    return out


def fold(square):
    rows, columns = square.shape
    tall = jnp.sum(square.reshape(rows // 8, 8, columns), axis=0)
    return functools.reduce(
        lambda a, b: a + b, [tall[:, i : i + 128] for i in range(0, columns, 128)]
    )


def kernel(
    n, step_rows, col_chunks,
    shape_ref, owner_ref, grads_ref, moment_ref, factor_ref, out_ref,
    outbound, g_full, own, other_rows, other_cols, half, s_rows, s_cols,
    r_rows, r_cols, adam_out, adam_in, sq_out, sq_in,
    own_sem, g_send, g_recv, a_send, a_recv, q_send, q_recv,
    zr_send, zr_recv, zc_send, zc_recv, sr_send, sr_recv, sc_send, sc_recv,
):
    count, band, width = grads_ref.shape
    me = lax.axis_index("fsdp")
    rep = lax.axis_index("rep")
    parity = rep % 2
    partner = rep + 1 - 2 * parity
    col_width = width // col_chunks
    row_chunks = width // step_rows
    group = step_rows // band
    first = rep * count

    barrier = pltpu.get_barrier_semaphore()

    @pl.loop(1, n)
    def _(t):
        pl.semaphore_signal(
            barrier, inc=1, device_id=(flipped(me, t, n), rep), device_id_type=MESH
        )

    pl.semaphore_signal(barrier, inc=1, device_id=(me, partner), device_id_type=MESH)

    own_copy = pltpu.make_async_copy(factor_ref.at[0, 0], own, own_sem)
    own_copy.start()

    def rows_of(index):
        return pl.ds(pl.multiple_of(index * band, band), band)

    line = me * band + lax.broadcasted_iota(jnp.int32, (band, width), 0)
    column = lax.broadcasted_iota(jnp.int32, (band, width), 1)
    masked = []
    for b in range(count):
        inside = (line < shape_ref[first + b, 0]) & (column < shape_ref[first + b, 1])
        wide = jnp.where(inside, grads_ref[b].astype(jnp.float32), 0.0)
        out_ref[b] = wide.astype(jnp.bfloat16)

    def fill(d):
        slot = jnp.zeros((band, width), jnp.bfloat16)
        for b in range(count):
            slot = jnp.where(owner_ref[first + b] == d, out_ref[b], slot)
        return slot

    @pl.loop(0, n)
    def _(d):
        outbound[d] = fill(d)

    g_full[rows_of(me)] = outbound[me]

    pl.semaphore_wait(barrier, n)

    def z_rows(s):
        chunk = flipped(me // group, row_chunks - 1 - s, row_chunks)
        rows = pl.ds(pl.multiple_of(chunk * step_rows, step_rows), step_rows)
        return pltpu.make_async_remote_copy(
            src_ref=factor_ref.at[0, 0, rows], dst_ref=other_rows.at[rows],
            send_sem=zr_send.at[s], recv_sem=zr_recv.at[s],
            device_id=(me, partner), device_id_type=MESH,
        )

    def z_cols(c):
        columns = pl.ds(c * col_width, col_width)
        return pltpu.make_async_remote_copy(
            src_ref=factor_ref.at[0, 0, :, columns], dst_ref=other_cols.at[c],
            send_sem=zc_send.at[c], recv_sem=zc_recv.at[c],
            device_id=(me, partner), device_id_type=MESH,
        )

    @pl.when(parity == 1)
    def _():
        for s in range(row_chunks):
            z_rows(s).start()

    @pl.when(parity == 0)
    def _():
        for c in range(col_chunks):
            z_cols(c).start()

    def peer_copy(source, target, send, recv, peer):
        return pltpu.make_async_remote_copy(
            src_ref=source, dst_ref=target, send_sem=send, recv_sem=recv,
            device_id=(peer, rep), device_id_type=MESH,
        )

    def g_copy(t, landing):
        peer = flipped(me, t, n)
        return peer_copy(
            outbound.at[peer], g_full.at[rows_of(landing)], g_send.at[t], g_recv.at[t], peer
        )

    @pl.loop(1, n)
    def _(s):
        g_copy(n - s, me).start()

    for b in range(count):
        adam = out_ref[b].astype(jnp.float32) / (
            jnp.sqrt(moment_ref[b].astype(jnp.float32)) + ADAM_EPS
        )
        adam_out[b] = fold(adam * adam)
    adam_in[me] = adam_out[...]

    def a_copy(t, landing):
        peer = flipped(me, t, n)
        return peer_copy(adam_out, adam_in.at[landing], a_send.at[t], a_recv.at[t], peer)

    def q_copy(t, landing):
        peer = flipped(me, t, n)
        return peer_copy(sq_out, sq_in.at[landing], q_send.at[t], q_recv.at[t], peer)

    @pl.loop(1, n)
    def _(t):
        a_copy(t, me).start()

    team_rows = jnp.int32(0)
    team_cols = jnp.int32(0)
    for b in range(count):
        mine = owner_ref[first + b] == me
        team_rows += jnp.where(mine, shape_ref[first + b, 0], 0)
        team_cols += jnp.where(mine, shape_ref[first + b, 1], 0)

    def clipped(full, row0, col0):
        r = row0 + lax.broadcasted_iota(jnp.int32, full.shape, 0)
        c = col0 + lax.broadcasted_iota(jnp.int32, full.shape, 1)
        return jnp.where((r < team_rows) & (c < team_cols), full, 0.0).astype(jnp.bfloat16)

    own_copy.wait()

    def sr_copy(t, landing):
        peer = flipped(me, t, n)
        return peer_copy(
            s_rows.at[rows_of(peer)], r_rows.at[landing], sr_send.at[t], sr_recv.at[t], peer
        )

    def sc_copy(t, c, landing):
        peer = flipped(me, t, n)
        return peer_copy(
            s_cols.at[c, rows_of(peer)], r_cols.at[landing, c],
            sc_send.at[t, c], sc_recv.at[t, c], peer,
        )

    @pl.when(parity == 0)
    def _():
        @pl.loop(0, n)
        def _(t):
            source = flipped(me, t, n)

            @pl.when(t != 0)
            def _():
                g_copy(t, source).wait_recv()

            half[rows_of(source)] = jnp.dot(
                g_full[rows_of(source)], own[...], preferred_element_type=jnp.float32
            ).astype(jnp.bfloat16)

        sq_out[...] = jnp.zeros_like(sq_out)

        @pl.loop(0, row_chunks)
        def _(s):
            z_rows(s).wait_recv()
            chunk = flipped(me // group, row_chunks - 1 - s, row_chunks)
            row0 = pl.multiple_of(chunk * step_rows, step_rows)
            full = jnp.dot(
                other_rows[pl.ds(row0, step_rows)], half[...],
                preferred_element_type=jnp.float32,
            )
            part = clipped(full, row0, 0)
            s_rows[pl.ds(row0, step_rows)] = part
            for i in range(group):
                t = (row_chunks - 1 - s) * group + i

                @pl.when(t != 0)
                def _():
                    sr_copy(t, me).start()

            wide = part.astype(jnp.float32)
            sq_out[...] += fold(wide * wide)

        r_rows[me] = s_rows[rows_of(me)]

    @pl.when(parity == 1)
    def _():
        @pl.loop(1, n)
        def _(t):
            g_copy(t, flipped(me, t, n)).wait_recv()

        sq_out[...] = jnp.zeros_like(sq_out)

        @pl.loop(0, col_chunks)
        def _(c):
            pltpu.make_async_remote_copy(
                src_ref=other_cols.at[c], dst_ref=other_cols.at[c],
                send_sem=zc_send.at[c], recv_sem=zc_recv.at[c],
                device_id=(me, partner), device_id_type=MESH,
            ).wait_recv()
            h = jnp.dot(
                g_full[...], other_cols[c], preferred_element_type=jnp.float32
            ).astype(jnp.bfloat16)
            full = jnp.dot(own[...], h, preferred_element_type=jnp.float32)
            part = clipped(full, 0, c * col_width)
            s_cols[c] = part

            @pl.loop(1, n)
            def _(s):
                sc_copy(n - s, c, me).start()

            wide = part.astype(jnp.float32)
            sq_out[...] += fold(wide * wide)
            r_cols[me, c] = s_cols[c, rows_of(me)]

    @pl.loop(1, n)
    def _(t):
        q_copy(t, me).start()

    sq_in[me] = sq_out[...]

    @pl.loop(1, n)
    def _(t):
        a_copy(t, flipped(me, t, n)).wait_recv()

    adam_sum = jnp.sum(adam_in[...], axis=0)

    @pl.loop(1, n)
    def _(t):
        q_copy(t, flipped(me, t, n)).wait_recv()

    ratios = []
    for b in range(count):
        adam_sq = jnp.sum(adam_sum[b], keepdims=True)
        shampoo_sq = jnp.sum(sq_in[owner_ref[first + b]], keepdims=True)
        ratios.append(jnp.sqrt(adam_sq) / jnp.sqrt(shampoo_sq + NORM_EPS))

    @pl.when(parity == 0)
    def _():
        @pl.loop(1, n)
        def _(t):
            sr_copy(t, flipped(me, t, n)).wait_recv()

        for b in range(count):
            wide = r_rows[owner_ref[first + b]].astype(jnp.float32)
            out_ref[b] = (wide * ratios[b]).astype(jnp.bfloat16)

        @pl.loop(1, n)
        def _(t):
            sr_copy(t, me).wait_send()

        for c in range(col_chunks):
            z_cols(c).wait_send()

    @pl.when(parity == 1)
    def _():
        @pl.loop(1, n)
        def _(t):
            for c in range(col_chunks):
                sc_copy(t, c, flipped(me, t, n)).wait_recv()

        for b in range(count):
            for c in range(col_chunks):
                wide = r_cols[owner_ref[first + b], c].astype(jnp.float32)
                out_ref[b, :, c * col_width : (c + 1) * col_width] = (
                    wide * ratios[b]
                ).astype(jnp.bfloat16)

        @pl.loop(1, n)
        def _(t):
            for c in range(col_chunks):
                sc_copy(t, c, me).wait_send()

        for s in range(row_chunks):
            z_rows(s).wait_send()

    @pl.loop(1, n)
    def _(t):
        g_copy(t, me).wait_send()
        a_copy(t, me).wait_send()
        q_copy(t, me).wait_send()


def on_device(grads, second_moment, root_factors, block_shape, block_owner):
    count, band, width = grads.shape
    n = lax.axis_size("fsdp")
    step_rows = max(band, 128)
    col_chunks = 8 if n <= 8 else 2
    row_chunks = width // step_rows
    col_width = width // col_chunks
    vmem = pl.BlockSpec(memory_space=pltpu.VMEM)
    smem = pl.BlockSpec(memory_space=pltpu.SMEM)
    bf16, f32 = jnp.bfloat16, jnp.float32
    dma = pltpu.SemaphoreType.DMA
    return pl.pallas_call(
        functools.partial(kernel, n, step_rows, col_chunks),
        out_shape=jax.ShapeDtypeStruct(grads.shape, bf16),
        in_specs=[smem, smem, vmem, vmem, pl.BlockSpec(memory_space=pl.ANY)],
        out_specs=vmem,
        scratch_shapes=[
            pltpu.VMEM((n, band, width), bf16),
            pltpu.VMEM((width, width), bf16),
            pltpu.VMEM((width, width), bf16),
            pltpu.VMEM((width, width), bf16),
            pltpu.VMEM((col_chunks, width, col_width), bf16),
            pltpu.VMEM((width, width), bf16),
            pltpu.VMEM((width, width), bf16),
            pltpu.VMEM((col_chunks, width, col_width), bf16),
            pltpu.VMEM((n, band, width), bf16),
            pltpu.VMEM((n, col_chunks, band, col_width), bf16),
            pltpu.VMEM((count, 8, 128), f32),
            pltpu.VMEM((n, count, 8, 128), f32),
            pltpu.VMEM((8, 128), f32),
            pltpu.VMEM((n, 8, 128), f32),
            dma,
            dma((n,)), dma((n,)), dma((n,)), dma((n,)), dma((n,)), dma((n,)),
            dma((row_chunks,)), dma((row_chunks,)),
            dma((col_chunks,)), dma((col_chunks,)),
            dma((n,)), dma((n,)),
            dma((n, col_chunks)), dma((n, col_chunks)),
        ],
        compiler_params=pltpu.CompilerParams(
            collective_id=0, has_side_effects=True, vmem_limit_bytes=44 * 1024 * 1024
        ),
        cost_estimate=pl.CostEstimate(
            flops=4 * width**3, bytes_accessed=4 * 1024 * 1024, transcendentals=0
        ),
    )(block_shape, block_owner, grads, second_moment, root_factors)


def solution(mesh):
    placed = (
        P("rep", "fsdp", None),
        P("rep", "fsdp", None),
        P("rep", "fsdp", None, None),
        P(),
        P(),
    )
    return jax.shard_map(
        on_device, mesh=mesh, in_specs=placed, out_specs=P("rep", "fsdp", None), check_vma=False
    )
```

time: 192 us -> 65.5 us (0.34)
  waiting for transfers between devices: 106 us -> 0 us
  Pallas kernels: 0 us -> 59.3 us
  blocking collectives: 48.8 us -> 0 us
  starting transfers between devices: 13.9 us -> 0 us
  other arithmetic: 7.96 us -> 0 us
  matrix products: 7.27 us -> 0 us
  local copies, waits for them, and re-layouts: 8.05 us -> 5.88 us
    pallas_call x0 -> x1, Pallas kernels: none -> 59.3 us  [on_device(): pl.pallas_call(functools.partial(kernel, n, step_rows, col_chunks), out_s...]
    ppermute x3 -> x0, waiting for transfers between devices: 55.8 us -> none  [shifted(): return lax.ppermute(block, axis, route)]
    all_to_all x2 -> x0, waiting for transfers between devices: 49.8 us -> none  [the longest x1 26.6 us: on_device(): lax.all_to_all(outbound, 'fsdp', split_axis=0, concat_axis=1, tiled=True)]
    psum x1 -> x0, blocking collectives: 48.8 us -> none  [on_device(): shampoo_all = lax.psum(spread_sq, ('fsdp', 'rep'))]
    all_to_all x2 -> x0, starting transfers between devices: 8.69 us -> none  [the longest x1 4.81 us: on_device(): lax.all_to_all(product.reshape(owners, band, width), 'fsdp', split_axis=0...]
    dot_general x3 -> x0, matrix products: 7.27 us -> none  [the longest x1 4.55 us: right_product(): jnp.dot(gathered, factor, preferred_element_type=jnp.float32)]
    unnamed x2 -> x10, local copies, waits for them, and re-layouts: 0.01 us -> 5.88 us
    ppermute x3 -> x0, starting transfers between devices: 5.23 us -> none  [shifted(): return lax.ppermute(block, axis, route)]
  transfers between devices with their start and end apart: 5 -> 0, of which waited for: 4 -> 0; matrix products, arithmetic and copies ran while one was open for 3% -> 0% of each run, Pallas kernels for 0% -> 0%
where the time goes in v1:
time: 65.5 us; the launch traced here: 65.2 us
  Pallas kernels  59.3 us (91%)
  local copies, waits for them, and re-layouts  5.88 us (9%)
    pallas_call x1, Pallas kernels, on_device(): pl.pallas_call(functools.partial(kernel, n, step_rows, col_chunks), out_s...  59.3 us
    unnamed x10, local copies, waits for them, and re-layouts  5.88 us

profile of v1, /device:TPU:0, one launch (start us, length us, event | category | flops | bytes accessed | tf_op | source)
XLA Modules:
  0.0 65.2 jit_solution(18433486711628367362)
XLA Ops:
  0.0 0.8 %copy.6.shape_ref = s32[8,2]{1,0:T(8,128)S(1)} copy(s32[8,2]{0,1:T(2,128)} %param.8) | data formatting | bytes 128 | tf_op args[3]
  0.8 0.0 copy-start
  0.8 1.6 %copy-done = bf16[1,1,1024,1024]{3,2,1,0:T(8,128)(2,1)S(1)} copy-done((bf16[1,1,1024,1024]{3,2,1,0:T(8,128)(2,1)S(1)}, bf16[1,1,1024,1024]{3,2,1,0:T(8,128)(2,1)}, u32[]{:S(2)}) %copy-start) | copy-done | bytes 2097176
  2.3 0.0 copy-start.1
  2.3 1.0 %copy-done.1 = bf16[2,128,1024]{2,1,0:T(8,128)(2,1)S(1)} copy-done((bf16[2,128,1024]{2,1,0:T(8,128)(2,1)S(1)}, bf16[2,128,1024]{2,1,0:T(8,128)(2,1)}, u32[]{:S(2)}) %copy-start.1) | copy-done | bytes 524312
  3.4 0.0 copy-start.2
  3.4 1.0 %copy-done.2 = bf16[2,128,1024]{2,1,0:T(8,128)(2,1)S(1)} copy-done((bf16[2,128,1024]{2,1,0:T(8,128)(2,1)S(1)}, bf16[2,128,1024]{2,1,0:T(8,128)(2,1)}, u32[]{:S(2)}) %copy-start.2) | copy-done | bytes 524312
  4.4 0.0 copy-start.3
  4.4 0.7 %copy-done.3 = s32[8]{0:T(128)S(1)} copy-done((s32[8]{0:T(128)S(1)}, s32[8]{0:T(128)}, u32[]{:S(2)}) %copy-start.3) | copy-done | bytes 56
  5.1 59.3 %shard_map.55 = bf16[2,128,1024]{2,1,0:T(8,128)(2,1)S(1)} custom-call(s32[8,2]{1,0:T(8,128)S(1)} %copy.6.shape_ref, s32[8]{0:T(128)S(1)} %copy-done.3, bf16[2,128,1024]{2,1,0:T(8,128)(2,1)S(1)} %copy-done.1, bf16[2,128,1024]{2,1,0:T(8,128)(2,1)S(1)} %copy-done.2, bf16[1,1,1024,1024]{3,2,1,0:T(8,128)(2,1)S(1)} %copy-done), custom_call_target="tpu_custom_call" | custom-call | flops 4294967296 | bytes 4194304 | tf_op jit(solution)/shard_map/pallas_call | solution.py:324
  64.4 0.8 %copy.8 = bf16[2,128,1024]{2,1,0:T(8,128)(2,1)} copy(bf16[2,128,1024]{2,1,0:T(8,128)(2,1)S(1)} %shard_map.55) | data formatting | bytes 1048576
Async XLA Ops:
  0.8 1.6 %copy-start = (bf16[1,1,1024,1024]{3,2,1,0:T(8,128)(2,1)S(1)}, bf16[1,1,1024,1024]{3,2,1,0:T(8,128)(2,1)}, u32[]{:S(2)}) copy-start(bf16[1,1,1024,1024]{3,2,1,0:T(8,128)(2,1)} %factor_ref.1) | copy-start | bytes 6291460
  2.3 1.0 %copy-start.1 = (bf16[2,128,1024]{2,1,0:T(8,128)(2,1)S(1)}, bf16[2,128,1024]{2,1,0:T(8,128)(2,1)}, u32[]{:S(2)}) copy-start(bf16[2,128,1024]{2,1,0:T(8,128)(2,1)} %grads_ref.1) | copy-start | bytes 1572868
  3.4 1.0 %copy-start.2 = (bf16[2,128,1024]{2,1,0:T(8,128)(2,1)S(1)}, bf16[2,128,1024]{2,1,0:T(8,128)(2,1)}, u32[]{:S(2)}) copy-start(bf16[2,128,1024]{2,1,0:T(8,128)(2,1)} %moment_ref.1) | copy-start | bytes 1572868
  4.4 0.7 %copy-start.3 = (s32[8]{0:T(128)S(1)}, s32[8]{0:T(128)}, u32[]{:S(2)}) copy-start(s32[8]{0:T(128)} %owner_ref.1) | copy-start | bytes 100

commit v2 on v1

--- a/solution.py
+++ b/solution.py
@@ -30,7 +30,8 @@
 
 def kernel(
     n, step_rows, col_chunks,
-    shape_ref, owner_ref, grads_ref, moment_ref, factor_ref, out_ref,
+    shape_hbm, owner_hbm, grads_hbm, moment_hbm, factor_ref, out_ref,
+    shape_ref, owner_ref, grads_ref, moment_ref, load_sem,
     outbound, g_full, own, other_rows, other_cols, half, s_rows, s_cols,
     r_rows, r_cols, adam_out, adam_in, sq_out, sq_in,
     own_sem, g_send, g_recv, a_send, a_recv, q_send, q_recv,
@@ -56,31 +57,20 @@
 
     pl.semaphore_signal(barrier, inc=1, device_id=(me, partner), device_id_type=MESH)
 
+    loads = [
+        pltpu.make_async_copy(source, target, load_sem.at[i])
+        for i, (source, target) in enumerate([
+            (shape_hbm, shape_ref), (owner_hbm, owner_ref),
+            (grads_hbm, grads_ref), (moment_hbm, moment_ref),
+        ])
+    ]
+    for load in loads:
+        load.start()
     own_copy = pltpu.make_async_copy(factor_ref.at[0, 0], own, own_sem)
     own_copy.start()
 
     def rows_of(index):
         return pl.ds(pl.multiple_of(index * band, band), band)
-
-    line = me * band + lax.broadcasted_iota(jnp.int32, (band, width), 0)
-    column = lax.broadcasted_iota(jnp.int32, (band, width), 1)
-    masked = []
-    for b in range(count):
-        inside = (line < shape_ref[first + b, 0]) & (column < shape_ref[first + b, 1])
-        wide = jnp.where(inside, grads_ref[b].astype(jnp.float32), 0.0)
-        out_ref[b] = wide.astype(jnp.bfloat16)
-
-    def fill(d):
-        slot = jnp.zeros((band, width), jnp.bfloat16)
-        for b in range(count):
-            slot = jnp.where(owner_ref[first + b] == d, out_ref[b], slot)
-        return slot
-
-    @pl.loop(0, n)
-    def _(d):
-        outbound[d] = fill(d)
-
-    g_full[rows_of(me)] = outbound[me]
 
     pl.semaphore_wait(barrier, n)
 
@@ -111,6 +101,29 @@
         for c in range(col_chunks):
             z_cols(c).start()
 
+    for load in loads[:3]:
+        load.wait()
+
+    line = me * band + lax.broadcasted_iota(jnp.int32, (band, width), 0)
+    column = lax.broadcasted_iota(jnp.int32, (band, width), 1)
+    masked = []
+    for b in range(count):
+        inside = (line < shape_ref[0, first + b]) & (column < shape_ref[1, first + b])
+        wide = jnp.where(inside, grads_ref[b].astype(jnp.float32), 0.0)
+        out_ref[b] = wide.astype(jnp.bfloat16)
+
+    def fill(d):
+        slot = jnp.zeros((band, width), jnp.bfloat16)
+        for b in range(count):
+            slot = jnp.where(owner_ref[first + b] == d, out_ref[b], slot)
+        return slot
+
+    @pl.loop(0, n)
+    def _(d):
+        outbound[d] = fill(d)
+
+    g_full[rows_of(me)] = outbound[me]
+
     def peer_copy(source, target, send, recv, peer):
         return pltpu.make_async_remote_copy(
             src_ref=source, dst_ref=target, send_sem=send, recv_sem=recv,
@@ -127,6 +140,8 @@
     def _(s):
         g_copy(n - s, me).start()
 
+    loads[3].wait()
+
     for b in range(count):
         adam = out_ref[b].astype(jnp.float32) / (
             jnp.sqrt(moment_ref[b].astype(jnp.float32)) + ADAM_EPS
@@ -150,8 +165,8 @@
     team_cols = jnp.int32(0)
     for b in range(count):
         mine = owner_ref[first + b] == me
-        team_rows += jnp.where(mine, shape_ref[first + b, 0], 0)
-        team_cols += jnp.where(mine, shape_ref[first + b, 1], 0)
+        team_rows += jnp.where(mine, shape_ref[0, first + b], 0)
+        team_cols += jnp.where(mine, shape_ref[1, first + b], 0)
 
     def clipped(full, row0, col0):
         r = row0 + lax.broadcasted_iota(jnp.int32, full.shape, 0)
@@ -317,16 +332,19 @@
     col_chunks = 8 if n <= 8 else 2
     row_chunks = width // step_rows
     col_width = width // col_chunks
-    vmem = pl.BlockSpec(memory_space=pltpu.VMEM)
-    smem = pl.BlockSpec(memory_space=pltpu.SMEM)
     bf16, f32 = jnp.bfloat16, jnp.float32
     dma = pltpu.SemaphoreType.DMA
     return pl.pallas_call(
         functools.partial(kernel, n, step_rows, col_chunks),
         out_shape=jax.ShapeDtypeStruct(grads.shape, bf16),
-        in_specs=[smem, smem, vmem, vmem, pl.BlockSpec(memory_space=pl.ANY)],
-        out_specs=vmem,
+        in_specs=[pl.BlockSpec(memory_space=pltpu.HBM)] * 5,
+        out_specs=pl.BlockSpec(memory_space=pltpu.VMEM),
         scratch_shapes=[
+            pltpu.SMEM((2, block_shape.shape[0]), jnp.int32),
+            pltpu.SMEM(block_owner.shape, jnp.int32),
+            pltpu.VMEM(grads.shape, bf16),
+            pltpu.VMEM(grads.shape, bf16),
+            dma((4,)),
             pltpu.VMEM((n, band, width), bf16),
             pltpu.VMEM((width, width), bf16),
             pltpu.VMEM((width, width), bf16),
@@ -349,12 +367,12 @@
             dma((n, col_chunks)), dma((n, col_chunks)),
         ],
         compiler_params=pltpu.CompilerParams(
-            collective_id=0, has_side_effects=True, vmem_limit_bytes=44 * 1024 * 1024
+            collective_id=0, has_side_effects=True, vmem_limit_bytes=60 * 1024 * 1024
         ),
         cost_estimate=pl.CostEstimate(
             flops=4 * width**3, bytes_accessed=4 * 1024 * 1024, transcendentals=0
         ),
-    )(block_shape, block_owner, grads, second_moment, root_factors)
+    )(block_shape.T, block_owner, grads, second_moment, root_factors)
 
 
 def solution(mesh):

time: 65.5 us -> 61.7 us (0.942)
  local copies, waits for them, and re-layouts: 5.88 us -> 1.87 us
    unnamed x10 -> x1, local copies, waits for them, and re-layouts: 5.88 us -> 1.87 us
where the time goes in v2:
time: 61.7 us; the launch traced here: 61.6 us
  Pallas kernels  59.7 us (97%)
  local copies, waits for them, and re-layouts  1.87 us (3%)
    pallas_call x1, Pallas kernels, on_device(): pl.pallas_call(functools.partial(kernel, n, step_rows, col_chunks), out_s...  59.7 us
    unnamed x1, local copies, waits for them, and re-layouts  1.87 us

profile of v2, /device:TPU:0, one launch (start us, length us, event | category | flops | bytes accessed | tf_op | source)
XLA Modules:
  0.0 61.6 jit_solution(17864314274020452322)
XLA Ops:
  0.0 59.7 %shard_map.55 = bf16[2,128,1024]{2,1,0:T(8,128)(2,1)} custom-call(s32[2,8]{1,0:T(2,128)} %bitcast.1, s32[8]{0:T(128)} %owner_hbm.1, bf16[2,128,1024]{2,1,0:T(8,128)(2,1)} %grads_hbm.1, bf16[2,128,1024]{2,1,0:T(8,128)(2,1)} %moment_hbm.1, bf16[1,1,1024,1024]{3,2,1,0:T(8,128)(2,1)} %factor_ref.1), custom_call_target="tpu_custom_call" | custom-call | flops 4294967296 | bytes 4194304 | tf_op jit(solution)/shard_map/pallas_call | solution.py:337
  59.7 1.9 %copy.7 = bf16[2,128,1024]{2,1,0:T(8,128)(2,1)} copy(bf16[2,128,1024]{2,1,0:T(8,128)(2,1)} %shard_map.55) | data formatting | bytes 1048576

commit v3 on v2

--- a/solution.py
+++ b/solution.py
@@ -45,6 +45,7 @@
     col_width = width // col_chunks
     row_chunks = width // step_rows
     group = step_rows // band
+    near = n // 2
     first = rep * count
 
     barrier = pltpu.get_barrier_semaphore()
@@ -72,35 +73,6 @@
     def rows_of(index):
         return pl.ds(pl.multiple_of(index * band, band), band)
 
-    pl.semaphore_wait(barrier, n)
-
-    def z_rows(s):
-        chunk = flipped(me // group, row_chunks - 1 - s, row_chunks)
-        rows = pl.ds(pl.multiple_of(chunk * step_rows, step_rows), step_rows)
-        return pltpu.make_async_remote_copy(
-            src_ref=factor_ref.at[0, 0, rows], dst_ref=other_rows.at[rows],
-            send_sem=zr_send.at[s], recv_sem=zr_recv.at[s],
-            device_id=(me, partner), device_id_type=MESH,
-        )
-
-    def z_cols(c):
-        columns = pl.ds(c * col_width, col_width)
-        return pltpu.make_async_remote_copy(
-            src_ref=factor_ref.at[0, 0, :, columns], dst_ref=other_cols.at[c],
-            send_sem=zc_send.at[c], recv_sem=zc_recv.at[c],
-            device_id=(me, partner), device_id_type=MESH,
-        )
-
-    @pl.when(parity == 1)
-    def _():
-        for s in range(row_chunks):
-            z_rows(s).start()
-
-    @pl.when(parity == 0)
-    def _():
-        for c in range(col_chunks):
-            z_cols(c).start()
-
     for load in loads[:3]:
         load.wait()
 
@@ -124,6 +96,41 @@
 
     g_full[rows_of(me)] = outbound[me]
 
+    pl.semaphore_wait(barrier, n)
+
+    def turn(s):
+        if row_chunks != 8:
+            return row_chunks - 1 - s
+        late = s // 6
+        return (1 - late) * (7 - 2 * (s % 3) - s // 3) + late * (7 - s)
+
+    def z_rows(s):
+        chunk = flipped(me // group, turn(s), row_chunks)
+        rows = pl.ds(pl.multiple_of(chunk * step_rows, step_rows), step_rows)
+        return pltpu.make_async_remote_copy(
+            src_ref=factor_ref.at[0, 0, rows], dst_ref=other_rows.at[rows],
+            send_sem=zr_send.at[s], recv_sem=zr_recv.at[s],
+            device_id=(me, partner), device_id_type=MESH,
+        )
+
+    def z_cols(c):
+        columns = pl.ds(c * col_width, col_width)
+        return pltpu.make_async_remote_copy(
+            src_ref=factor_ref.at[0, 0, :, columns], dst_ref=other_cols.at[c],
+            send_sem=zc_send.at[c], recv_sem=zc_recv.at[c],
+            device_id=(me, partner), device_id_type=MESH,
+        )
+
+    @pl.when(parity == 1)
+    def _():
+        for s in range(row_chunks):
+            z_rows(s).start()
+
+    @pl.when(parity == 0)
+    def _():
+        for c in range(col_chunks):
+            z_cols(c).start()
+
     def peer_copy(source, target, send, recv, peer):
         return pltpu.make_async_remote_copy(
             src_ref=source, dst_ref=target, send_sem=send, recv_sem=recv,
@@ -207,7 +214,7 @@
         @pl.loop(0, row_chunks)
         def _(s):
             z_rows(s).wait_recv()
-            chunk = flipped(me // group, row_chunks - 1 - s, row_chunks)
+            chunk = flipped(me // group, turn(s), row_chunks)
             row0 = pl.multiple_of(chunk * step_rows, step_rows)
             full = jnp.dot(
                 other_rows[pl.ds(row0, step_rows)], half[...],
@@ -216,7 +223,7 @@
             part = clipped(full, row0, 0)
             s_rows[pl.ds(row0, step_rows)] = part
             for i in range(group):
-                t = (row_chunks - 1 - s) * group + i
+                t = turn(s) * group + i
 
                 @pl.when(t != 0)
                 def _():
@@ -245,16 +252,21 @@
             h = jnp.dot(
                 g_full[...], other_cols[c], preferred_element_type=jnp.float32
             ).astype(jnp.bfloat16)
-            full = jnp.dot(own[...], h, preferred_element_type=jnp.float32)
-            part = clipped(full, 0, c * col_width)
-            s_cols[c] = part
-
-            @pl.loop(1, n)
-            def _(s):
-                sc_copy(n - s, c, me).start()
-
-            wide = part.astype(jnp.float32)
-            sq_out[...] += fold(wide * wide)
+            for far in (1, 0):
+                side = flipped(me // near, far, 2)
+                row0 = pl.multiple_of(side * (width // 2), width // 2)
+                rows = pl.ds(row0, width // 2)
+                full = jnp.dot(own[rows], h, preferred_element_type=jnp.float32)
+                part = clipped(full, row0, c * col_width)
+                s_cols[c, rows] = part
+
+                @pl.loop(1 - far, near)
+                def _(s):
+                    sc_copy((1 + far) * near - 1 - s + (1 - far), c, me).start()
+
+                wide = part.astype(jnp.float32)
+                sq_out[...] += fold(wide * wide)
+
             r_cols[me, c] = s_cols[c, rows_of(me)]
 
     @pl.loop(1, n)

time: 61.7 us -> 61.3 us (level)
  no operation moved by 1% of the time
where the time goes in v3:
time: 61.3 us; the launch traced here: 61.2 us
  Pallas kernels  59.3 us (97%)
  local copies, waits for them, and re-layouts  1.87 us (3%)
    pallas_call x1, Pallas kernels, on_device(): pl.pallas_call(functools.partial(kernel, n, step_rows, col_chunks), out_s...  59.3 us
    unnamed x1, local copies, waits for them, and re-layouts  1.87 us

profile of v3, /device:TPU:0, one launch (start us, length us, event | category | flops | bytes accessed | tf_op | source)
XLA Modules:
  0.0 61.2 jit_solution(12084182012845187358)
XLA Ops:
  0.0 59.3 %shard_map.55 = bf16[2,128,1024]{2,1,0:T(8,128)(2,1)} custom-call(s32[2,8]{1,0:T(2,128)} %bitcast.1, s32[8]{0:T(128)} %owner_hbm.1, bf16[2,128,1024]{2,1,0:T(8,128)(2,1)} %grads_hbm.1, bf16[2,128,1024]{2,1,0:T(8,128)(2,1)} %moment_hbm.1, bf16[1,1,1024,1024]{3,2,1,0:T(8,128)(2,1)} %factor_ref.1), custom_call_target="tpu_custom_call" | custom-call | flops 4294967296 | bytes 4194304 | tf_op jit(solution)/shard_map/pallas_call | solution.py:349
  59.3 1.9 %copy.7 = bf16[2,128,1024]{2,1,0:T(8,128)(2,1)} copy(bf16[2,128,1024]{2,1,0:T(8,128)(2,1)} %shard_map.55) | data formatting | bytes 1048576

commit v4 on v3

--- a/solution.py
+++ b/solution.py
@@ -236,22 +236,39 @@
 
     @pl.when(parity == 1)
     def _():
-        @pl.loop(1, n)
-        def _(t):
-            g_copy(t, flipped(me, t, n)).wait_recv()
-
-        sq_out[...] = jnp.zeros_like(sq_out)
-
-        @pl.loop(0, col_chunks)
-        def _(c):
+        def z_arrived(c):
             pltpu.make_async_remote_copy(
                 src_ref=other_cols.at[c], dst_ref=other_cols.at[c],
                 send_sem=zc_send.at[c], recv_sem=zc_recv.at[c],
                 device_id=(me, partner), device_id_type=MESH,
             ).wait_recv()
-            h = jnp.dot(
-                g_full[...], other_cols[c], preferred_element_type=jnp.float32
+
+        z_arrived(0)
+
+        @pl.loop(0, n)
+        def _(t):
+            source = flipped(me, t, n)
+
+            @pl.when(t != 0)
+            def _():
+                g_copy(t, source).wait_recv()
+
+            half[rows_of(source), 0:col_width] = jnp.dot(
+                g_full[rows_of(source)], other_cols[0], preferred_element_type=jnp.float32
             ).astype(jnp.bfloat16)
+
+        sq_out[...] = jnp.zeros_like(sq_out)
+
+        @pl.loop(0, col_chunks)
+        def _(c):
+            @pl.when(c != 0)
+            def _():
+                z_arrived(c)
+                half[:, 0:col_width] = jnp.dot(
+                    g_full[...], other_cols[c], preferred_element_type=jnp.float32
+                ).astype(jnp.bfloat16)
+
+            h = half[:, 0:col_width]
             for far in (1, 0):
                 side = flipped(me // near, far, 2)
                 row0 = pl.multiple_of(side * (width // 2), width // 2)

time: 61.3 us -> 61.3 us (level)
  no operation moved by 1% of the time
where the time goes in v4:
time: 61.3 us; the launch traced here: 61.2 us
  Pallas kernels  59.3 us (97%)
  local copies, waits for them, and re-layouts  1.87 us (3%)
    pallas_call x1, Pallas kernels, on_device(): pl.pallas_call(functools.partial(kernel, n, step_rows, col_chunks), out_s...  59.3 us
    unnamed x1, local copies, waits for them, and re-layouts  1.87 us

profile of v4, /device:TPU:0, one launch (start us, length us, event | category | flops | bytes accessed | tf_op | source)
XLA Modules:
  0.0 61.2 jit_solution(7572756064142391528)
XLA Ops:
  0.0 59.3 %shard_map.55 = bf16[2,128,1024]{2,1,0:T(8,128)(2,1)} custom-call(s32[2,8]{1,0:T(2,128)} %bitcast.1, s32[8]{0:T(128)} %owner_hbm.1, bf16[2,128,1024]{2,1,0:T(8,128)(2,1)} %grads_hbm.1, bf16[2,128,1024]{2,1,0:T(8,128)(2,1)} %moment_hbm.1, bf16[1,1,1024,1024]{3,2,1,0:T(8,128)(2,1)} %factor_ref.1), custom_call_target="tpu_custom_call" | custom-call | flops 4294967296 | bytes 4194304 | tf_op jit(solution)/shard_map/pallas_call | solution.py:366
  59.3 1.9 %copy.7 = bf16[2,128,1024]{2,1,0:T(8,128)(2,1)} copy(bf16[2,128,1024]{2,1,0:T(8,128)(2,1)} %shard_map.55) | data formatting | bytes 1048576
